TPU v7x, 32 devices: a whole 2x2x4 slice. The times are simulated.
32 devices in a mesh: sec: 2 (over core), grp: 4 (over y, x), blk: 4 (over z).
Axes of the slice: x: 2, y: 2, z: 4, core: 2. Of those that a mesh axis runs over, the one named last changes fastest.
Arguments:
- atm_flux: bfloat16 [2, 60, 65536], P(None, None, ('sec', 'grp', 'blk')), may hold values from -25 to 25
- tile_bank: bfloat16 [128, 128, 128], replicated, may hold values from -1 to 1
- pair_count: int32 [32], P(('sec', 'grp', 'blk')), may hold values from 32 to 128, as said below
- pair_source: int32 [4096], P(('sec', 'grp', 'blk')), may hold values from 0 to 15
- pair_tile: int32 [4096], P(('sec', 'grp', 'blk')), may hold values from 0 to 127
- pair_target: int32 [4096], P(('sec', 'grp', 'blk')), may hold values from 0 to 7
- tracers: bfloat16 [32, 60, 8192], P(None, None, ('sec', 'grp', 'blk')), may hold values from -6 to 6
- diffusivity: float32 [31, 8192], P(None, ('sec', 'grp', 'blk')), may hold values from 0.2 to 5
- column_depth: int32 [8192], P(('sec', 'grp', 'blk')), may hold values from 0 to 32
Outputs:
- mixed_tracers: float32 [32, 60, 8192], P(None, None, ('sec', 'grp', 'blk'))
Inputs may be any that keep to these rules, and one draw needn't show every extreme that they name: `pair_count`: pairs at positions 127 and below that are at or past a device's count are unused; some device has exactly 128 live pairs. `pair_target`: a target t names ocean block t % 2 of the device at blk index t // 2 with the same sec and grp. Levels at index column_depth and below are dry; 0 marks a land column.
All inputs are finite; a program needn't handle non-finite values.
Results may differ from a plain program's by a relative error of at most 0.013.
Values may be sent and summed in bfloat16 or wider, within the bound.
A program may use at most 64 MiB of HBM per device.

v0:
```python
import jax
import jax.numpy as jnp
from jax import lax
from jax.sharding import PartitionSpec as P

pair_group = 16


def column_factors(diffusivity, column_depth):
    layer_count = diffusivity.shape[0] + 1
    layer_ids = jnp.arange(layer_count, dtype=jnp.int32)
    active = layer_ids[:, None] < column_depth[None, :]
    interior = diffusivity * active[1:].astype(diffusivity.dtype)
    boundary = jnp.zeros_like(diffusivity[:1])
    coupling = jnp.concatenate([boundary, interior, boundary], axis=0)
    diagonal = 1.0 + coupling[:-1] + coupling[1:]
    inverse_pivot = []
    upper_ratio = []
    for k in range(layer_count):
        if k == 0:
            pivot_entry = diagonal[0]
        else:
            pivot_entry = diagonal[k] + coupling[k] * upper_ratio[k - 1]
        inverse = 1.0 / pivot_entry
        inverse_pivot.append(inverse)
        upper_ratio.append(-coupling[k + 1] * inverse)
    live_mask = active.astype(diffusivity.dtype)[:, None, :]
    surface = (column_depth > 0).astype(diffusivity.dtype)
    return (coupling, inverse_pivot, upper_ratio, live_mask, surface)


def mix_once(column_state, surface_term, factors):
    coupling, inverse_pivot, upper_ratio, live_mask, surface = factors
    right_side = column_state.at[0].add(surface_term * surface[None, :]) * live_mask
    forward = []
    for k in range(right_side.shape[0]):
        if k == 0:
            carried = right_side[0]
        else:
            carried = right_side[k] + coupling[k][None, :] * forward[k - 1]
        forward.append(carried * inverse_pivot[k][None, :])
    solved = [forward[-1]]
    for k in range(right_side.shape[0] - 2, -1, -1):
        solved.append(forward[k] - upper_ratio[k][None, :] * solved[-1])
    return jnp.stack(solved[::-1])


def merge_sources(arrived):
    return jnp.sum(arrived.astype(jnp.float32), axis=0)


def body(
    atm_flux,
    tile_bank,
    pair_count,
    pair_source,
    pair_tile,
    pair_target,
    tracers,
    diffusivity,
    column_depth,
):
    sub_count, field_count, atm_rows = atm_flux.shape
    tile_width = tile_bank.shape[1]
    source_blocks = atm_rows // tile_width
    columns = tracers.shape[2]
    ocean_blocks = columns // tile_width
    peer_count = lax.axis_size("blk")
    devices_all = lax.axis_size("sec") * lax.axis_size("grp") * peer_count
    stacked = sub_count * field_count
    flux_blocks = atm_flux.reshape(stacked, source_blocks, tile_width)
    live_count = pair_count[0]

    def add_group(group_index, slot_sums):
        first_pair = group_index * pair_group
        sources = lax.dynamic_slice_in_dim(pair_source, first_pair, pair_group)
        tile_ids = lax.dynamic_slice_in_dim(pair_tile, first_pair, pair_group)
        targets = lax.dynamic_slice_in_dim(pair_target, first_pair, pair_group)
        picked = jnp.take(flux_blocks, sources, axis=1)
        chosen = jnp.take(tile_bank, tile_ids, axis=0)
        products = jnp.einsum("sgr,grc->gsc", picked, chosen, preferred_element_type=jnp.float32)
        live_pairs = (first_pair + jnp.arange(pair_group, dtype=jnp.int32) < live_count).astype(
            jnp.float32
        )
        products = products * live_pairs[:, None, None]
        return slot_sums.at[targets // ocean_blocks, :, targets % ocean_blocks].add(products)

    zero_sums = jnp.zeros((peer_count, stacked, ocean_blocks, tile_width), jnp.float32)
    rounds = pair_source.shape[0] // pair_group
    outgoing = lax.fori_loop(0, rounds, add_group, zero_sums).astype(jnp.bfloat16)
    outgoing = outgoing.reshape(peer_count, sub_count, field_count, columns)
    atm_part = jnp.sum(atm_flux.astype(jnp.float32), axis=2)
    forcing = merge_sources(
        lax.all_to_all(outgoing, "blk", split_axis=0, concat_axis=0, tiled=True)
    )
    ocean_late = jnp.sum(forcing, axis=2)
    atm_total, ocean_total = lax.psum((atm_part, ocean_late), ("sec", "grp", "blk"))
    correction = (atm_total * (ocean_blocks / source_blocks) - ocean_total) / (
        columns * devices_all
    )
    factors = column_factors(diffusivity, column_depth)
    column_state = tracers.astype(jnp.float32)
    for substep in range(sub_count):
        column_state = mix_once(
            column_state, forcing[substep] + correction[substep][:, None], factors
        )
    return column_state


def solution(mesh):
    placed = (
        P(None, None, ("sec", "grp", "blk")),
        P(),
        P(("sec", "grp", "blk")),
        P(("sec", "grp", "blk")),
        P(("sec", "grp", "blk")),
        P(("sec", "grp", "blk")),
        P(None, None, ("sec", "grp", "blk")),
        P(None, ("sec", "grp", "blk")),
        P(("sec", "grp", "blk")),
    )
    return jax.shard_map(
        body,
        mesh=mesh,
        in_specs=placed,
        out_specs=P(None, None, ("sec", "grp", "blk")),
        check_vma=False,
    )
```

profile of v0, /device:TPU:0, one launch (start us, length us, event | category | flops | bytes accessed | tf_op | source)
XLA Modules:
  0.0 121.5 jit_solution(9731277089160563688)
XLA Ops:
  0.0 1.2 %copy.39 = bf16[2,60,2048]{2,1,0:T(8,128)(2,1)S(1)} copy(bf16[2,60,2048]{2,0,1:T(2,128)(2,1)} %param.15) | data formatting | bytes 983040 | tf_op args[0]
  1.7 54.9 %while.17 = (s32[]{:T(128)}, f32[4,120,2,128]{3,1,2,0:T(8,128)S(1)}, s32[128]{0:T(128)S(1)}, s32[128]{0:T(128)S(1)}, bf16[120,16,128]{2,0,1:T(8,128)(2,1)S(1)}, ...) while((s32[]{:T(128)}, ...), condition=%wide.region_2.3_spmd, body=%wide.region_0.2_spmd.sunk | while | flops 63916820 | bytes 6988919 | solution.py:90
  1.8 0.7 compare_and_fusion.4
  3.3 2.8 %gather_fusion = bf16[16,128,128]{2,1,0:T(8,128)(2,1)S(1)} fusion(bf16[128,128,128]{2,1,0:T(8,128)(2,1)} %get-tuple-element.546, s32[1024]{0:T(1024)S(1)} %pad_clamp_fusion.4), kind=kCustom, calls=%fused_computation.1.clone.1 | custom fusion | bytes 1048640 | tf_op jit(solution)/shard_map/while/body/eval_jaxpr/jit(_take)/gather | solution.py:80
  6.6 1.9 %scatter_fusion = f32[4,120,2,128]{3,1,2,0:T(8,128)S(1)} fusion(f32[4,120,2,128]{3,1,2,0:T(8,128)S(1)} %get-tuple-element.529, s32[16]{0:T(128)S(1)} %fusion.178, f32[16,120,128]{2,1,0:T(8,128)S(1)} %convolution_multiply_fusion.2), kind=kCustom, calls=%fused_computation.2.clone.1 | custom fusion | flops 245760 | bytes 2949248 | tf_op jit(solution)/shard_map/while/body/eval_jaxpr/scatter-add | solution.py:86
  8.7 0.7 compare_and_fusion.4
  10.2 2.8 %gather_fusion = bf16[16,128,128]{2,1,0:T(8,128)(2,1)S(1)} fusion(bf16[128,128,128]{2,1,0:T(8,128)(2,1)} %get-tuple-element.546, s32[1024]{0:T(1024)S(1)} %pad_clamp_fusion.4), kind=kCustom, calls=%fused_computation.1.clone.1 | custom fusion | bytes 1048640 | tf_op jit(solution)/shard_map/while/body/eval_jaxpr/jit(_take)/gather | solution.py:80
  13.5 1.9 %scatter_fusion = f32[4,120,2,128]{3,1,2,0:T(8,128)S(1)} fusion(f32[4,120,2,128]{3,1,2,0:T(8,128)S(1)} %get-tuple-element.529, s32[16]{0:T(128)S(1)} %fusion.178, f32[16,120,128]{2,1,0:T(8,128)S(1)} %convolution_multiply_fusion.2), kind=kCustom, calls=%fused_computation.2.clone.1 | custom fusion | flops 245760 | bytes 2949248 | tf_op jit(solution)/shard_map/while/body/eval_jaxpr/scatter-add | solution.py:86
  15.6 0.7 compare_and_fusion.4
  17.0 2.8 %gather_fusion = bf16[16,128,128]{2,1,0:T(8,128)(2,1)S(1)} fusion(bf16[128,128,128]{2,1,0:T(8,128)(2,1)} %get-tuple-element.546, s32[1024]{0:T(1024)S(1)} %pad_clamp_fusion.4), kind=kCustom, calls=%fused_computation.1.clone.1 | custom fusion | bytes 1048640 | tf_op jit(solution)/shard_map/while/body/eval_jaxpr/jit(_take)/gather | solution.py:80
  20.4 1.9 %scatter_fusion = f32[4,120,2,128]{3,1,2,0:T(8,128)S(1)} fusion(f32[4,120,2,128]{3,1,2,0:T(8,128)S(1)} %get-tuple-element.529, s32[16]{0:T(128)S(1)} %fusion.178, f32[16,120,128]{2,1,0:T(8,128)S(1)} %convolution_multiply_fusion.2), kind=kCustom, calls=%fused_computation.2.clone.1 | custom fusion | flops 245760 | bytes 2949248 | tf_op jit(solution)/shard_map/while/body/eval_jaxpr/scatter-add | solution.py:86
  22.4 0.7 compare_and_fusion.4
  23.9 2.8 %gather_fusion = bf16[16,128,128]{2,1,0:T(8,128)(2,1)S(1)} fusion(bf16[128,128,128]{2,1,0:T(8,128)(2,1)} %get-tuple-element.546, s32[1024]{0:T(1024)S(1)} %pad_clamp_fusion.4), kind=kCustom, calls=%fused_computation.1.clone.1 | custom fusion | bytes 1048640 | tf_op jit(solution)/shard_map/while/body/eval_jaxpr/jit(_take)/gather | solution.py:80
  27.2 1.9 %scatter_fusion = f32[4,120,2,128]{3,1,2,0:T(8,128)S(1)} fusion(f32[4,120,2,128]{3,1,2,0:T(8,128)S(1)} %get-tuple-element.529, s32[16]{0:T(128)S(1)} %fusion.178, f32[16,120,128]{2,1,0:T(8,128)S(1)} %convolution_multiply_fusion.2), kind=kCustom, calls=%fused_computation.2.clone.1 | custom fusion | flops 245760 | bytes 2949248 | tf_op jit(solution)/shard_map/while/body/eval_jaxpr/scatter-add | solution.py:86
  29.3 0.7 compare_and_fusion.4
  30.8 2.8 %gather_fusion = bf16[16,128,128]{2,1,0:T(8,128)(2,1)S(1)} fusion(bf16[128,128,128]{2,1,0:T(8,128)(2,1)} %get-tuple-element.546, s32[1024]{0:T(1024)S(1)} %pad_clamp_fusion.4), kind=kCustom, calls=%fused_computation.1.clone.1 | custom fusion | bytes 1048640 | tf_op jit(solution)/shard_map/while/body/eval_jaxpr/jit(_take)/gather | solution.py:80
  34.1 1.9 %scatter_fusion = f32[4,120,2,128]{3,1,2,0:T(8,128)S(1)} fusion(f32[4,120,2,128]{3,1,2,0:T(8,128)S(1)} %get-tuple-element.529, s32[16]{0:T(128)S(1)} %fusion.178, f32[16,120,128]{2,1,0:T(8,128)S(1)} %convolution_multiply_fusion.2), kind=kCustom, calls=%fused_computation.2.clone.1 | custom fusion | flops 245760 | bytes 2949248 | tf_op jit(solution)/shard_map/while/body/eval_jaxpr/scatter-add | solution.py:86
  36.1 0.7 compare_and_fusion.4
  37.6 2.8 %gather_fusion = bf16[16,128,128]{2,1,0:T(8,128)(2,1)S(1)} fusion(bf16[128,128,128]{2,1,0:T(8,128)(2,1)} %get-tuple-element.546, s32[1024]{0:T(1024)S(1)} %pad_clamp_fusion.4), kind=kCustom, calls=%fused_computation.1.clone.1 | custom fusion | bytes 1048640 | tf_op jit(solution)/shard_map/while/body/eval_jaxpr/jit(_take)/gather | solution.py:80
  41.0 1.9 %scatter_fusion = f32[4,120,2,128]{3,1,2,0:T(8,128)S(1)} fusion(f32[4,120,2,128]{3,1,2,0:T(8,128)S(1)} %get-tuple-element.529, s32[16]{0:T(128)S(1)} %fusion.178, f32[16,120,128]{2,1,0:T(8,128)S(1)} %convolution_multiply_fusion.2), kind=kCustom, calls=%fused_computation.2.clone.1 | custom fusion | flops 245760 | bytes 2949248 | tf_op jit(solution)/shard_map/while/body/eval_jaxpr/scatter-add | solution.py:86
  43.0 0.7 compare_and_fusion.4
  44.5 2.8 %gather_fusion = bf16[16,128,128]{2,1,0:T(8,128)(2,1)S(1)} fusion(bf16[128,128,128]{2,1,0:T(8,128)(2,1)} %get-tuple-element.546, s32[1024]{0:T(1024)S(1)} %pad_clamp_fusion.4), kind=kCustom, calls=%fused_computation.1.clone.1 | custom fusion | bytes 1048640 | tf_op jit(solution)/shard_map/while/body/eval_jaxpr/jit(_take)/gather | solution.py:80
  47.8 1.9 %scatter_fusion = f32[4,120,2,128]{3,1,2,0:T(8,128)S(1)} fusion(f32[4,120,2,128]{3,1,2,0:T(8,128)S(1)} %get-tuple-element.529, s32[16]{0:T(128)S(1)} %fusion.178, f32[16,120,128]{2,1,0:T(8,128)S(1)} %convolution_multiply_fusion.2), kind=kCustom, calls=%fused_computation.2.clone.1 | custom fusion | flops 245760 | bytes 2949248 | tf_op jit(solution)/shard_map/while/body/eval_jaxpr/scatter-add | solution.py:86
  49.9 0.7 compare_and_fusion.4
  51.3 2.8 %gather_fusion = bf16[16,128,128]{2,1,0:T(8,128)(2,1)S(1)} fusion(bf16[128,128,128]{2,1,0:T(8,128)(2,1)} %get-tuple-element.546, s32[1024]{0:T(1024)S(1)} %pad_clamp_fusion.4), kind=kCustom, calls=%fused_computation.1.clone.1 | custom fusion | bytes 1048640 | tf_op jit(solution)/shard_map/while/body/eval_jaxpr/jit(_take)/gather | solution.py:80
  54.7 1.9 %scatter_fusion = f32[4,120,2,128]{3,1,2,0:T(8,128)S(1)} fusion(f32[4,120,2,128]{3,1,2,0:T(8,128)S(1)} %get-tuple-element.529, s32[16]{0:T(128)S(1)} %fusion.178, f32[16,120,128]{2,1,0:T(8,128)S(1)} %convolution_multiply_fusion.2), kind=kCustom, calls=%fused_computation.2.clone.1 | custom fusion | flops 245760 | bytes 2949248 | tf_op jit(solution)/shard_map/while/body/eval_jaxpr/scatter-add | solution.py:86
  57.1 0.9 copy.42
  58.0 6.3 %all-to-all-start = ((bf16[4,2,60,256]{3,1,2,0:T(2,128)(2,1)}), bf16[4,2,60,256]{3,1,2,0:T(2,128)(2,1)S(1)}, u32[]{:S(2)}, u32[]{:S(2)}) async-start(bf16[4,2,60,256]{3,1,2,0:T(2,128)(2,1)} %copy.42), calls=%async_computation | async-start | bytes 491520 | tf_op jit(solution)/shard_map/all_to_all | solution.py:94
  69.5 3.3 %all-to-all-done = bf16[4,2,60,256]{3,1,2,0:T(2,128)(2,1)S(1)} async-done(((bf16[4,2,60,256]{3,1,2,0:T(2,128)(2,1)}), bf16[4,2,60,256]{3,1,2,0:T(2,128)(2,1)S(1)}, u32[]{:S(2)}, u32[]{:S(2)}) %all-to-all-start) | async-done | bytes 245792 | tf_op jit(solution)/shard_map/all_to_all | solution.py:94
  73.6 39.5 %all-reduce.2 = (f32[2,60]{0,1:T(8,128)S(1)}, f32[2,60]{0,1:T(8,128)S(1)}) all-reduce(f32[2,60]{0,1:T(8,128)S(1)} %copy.45, f32[2,60]{0,1:T(8,128)S(1)} %convert_reduce_fusion), channel_id=1, replica_groups=mesh['sec'=2,'grp'=4,'blk'=4] {'sec','grp','blk'}, use_global_device_ids=true, to_apply=%region_7.8 | all-reduce | flops 240 | bytes 1920 | tf_op jit(solution)/shard_map/psum | solution.py:97
  115.0 1.4 %constant_dynamic-update-slice_fusion.31 = (f32[32,60,256]{2,1,0:T(8,128)S(1)}, f32[1,60,256]{2,1,0:T(8,128)S(1)}, f32[1,60,256]{2,1,0:T(8,128)S(1)}, f32[1,60,2...) fusion(f32[256]{0:T(256)S(1)} %bitcast.182, ...), kind=kLoop, calls=%fused_computation.70 | loop fusion | flops 2396159 | bytes 4159488
  119.1 2.4 %copy.46 = f32[32,60,256]{2,0,1:T(8,128)} copy(f32[32,60,256]{2,1,0:T(8,128)S(1)} %constant_dynamic-update-slice_fusion.32) | data formatting | bytes 3932160 | tf_op jit(solution)/shard_map/stack | solution.py:45
  (291 shorter events, 20.8 us)
Async XLA Ops:
  0.0 1.7 %copy-start.70 = (s32[128]{0:T(128)S(1)}, s32[128]{0:T(128)}, u32[]{:S(2)}) copy-start(s32[128]{0:T(128)} %param.20) | copy-start | bytes 1540
  0.0 1.7 %copy-start.21 = (s32[128]{0:T(128)S(1)}, s32[128]{0:T(128)}, u32[]{:S(2)}) copy-start(s32[128]{0:T(128)} %param.19) | copy-start | bytes 1540
  0.0 1.7 %copy-start.22 = (s32[128]{0:T(128)S(1)}, s32[128]{0:T(128)}, u32[]{:S(2)}) copy-start(s32[128]{0:T(128)} %param.18) | copy-start | bytes 1540
  56.6 7.7 %copy-start.69 = (s32[256]{0:T(256)S(1)}, s32[256]{0:T(256)}, u32[]{:S(2)}) copy-start(s32[256]{0:T(256)} %param.23) | copy-start | bytes 3076
  56.6 8.2 %copy-start.2 = (f32[31,256]{1,0:T(8,128)S(1)}, f32[31,256]{1,0:T(8,128)}, u32[]{:S(2)}) copy-start(f32[31,256]{1,0:T(8,128)} %param.22) | copy-start | bytes 95236
  56.6 11.8 %copy-start = (bf16[2,60,2048]{2,0,1:T(2,128)(2,1)S(1)}, bf16[2,60,2048]{2,0,1:T(2,128)(2,1)}, u32[]{:S(2)}) copy-start(bf16[2,60,2048]{2,0,1:T(2,128)(2,1)} %param.15) | copy-start | bytes 1474564
  56.7 12.3 %copy-start.1 = (bf16[32,60,256]{2,0,1:T(8,128)(2,1)S(1)}, bf16[32,60,256]{2,0,1:T(8,128)(2,1)}, u32[]{:S(2)}) copy-start(bf16[32,60,256]{2,0,1:T(8,128)(2,1)} %param.21) | copy-start | bytes 2949124
  58.0 14.9 %all-to-all-start = ((bf16[4,2,60,256]{3,1,2,0:T(2,128)(2,1)}), bf16[4,2,60,256]{3,1,2,0:T(2,128)(2,1)S(1)}, u32[]{:S(2)}, u32[]{:S(2)}) async-start(bf16[4,2,60,256]{3,1,2,0:T(2,128)(2,1)} %copy.42), calls=%async_computation | async-start | bytes 491520 | tf_op jit(solution)/shard_map/all_to_all | solution.py:94
  64.9 2.8 %copy-start.3 = (f32[1,256]{1,0:T(1,128)}, f32[1,256]{1,0:T(1,128)S(1)}, u32[]{:S(2)}) copy-start(f32[1,256]{1,0:T(1,128)S(1)} %get-tuple-element.365) | copy-start | bytes 3076
  65.0 2.8 %copy-start.5 = (f32[1,256]{1,0:T(1,128)}, f32[1,256]{1,0:T(1,128)S(1)}, u32[]{:S(2)}) copy-start(f32[1,256]{1,0:T(1,128)S(1)} %get-tuple-element.368) | copy-start | bytes 3076
  65.0 2.7 %copy-start.7 = (f32[1,256]{1,0:T(1,128)}, f32[1,256]{1,0:T(1,128)S(1)}, u32[]{:S(2)}) copy-start(f32[1,256]{1,0:T(1,128)S(1)} %get-tuple-element.374) | copy-start | bytes 3076
  65.1 2.7 %copy-start.9 = (f32[1,256]{1,0:T(1,128)}, f32[1,256]{1,0:T(1,128)S(1)}, u32[]{:S(2)}) copy-start(f32[1,256]{1,0:T(1,128)S(1)} %get-tuple-element.377) | copy-start | bytes 3076
  65.1 2.7 %copy-start.11 = (f32[1,256]{1,0:T(1,128)}, f32[1,256]{1,0:T(1,128)S(1)}, u32[]{:S(2)}) copy-start(f32[1,256]{1,0:T(1,128)S(1)} %get-tuple-element.380) | copy-start | bytes 3076
  66.3 2.2 %copy-start.19 = (f32[1,256]{1,0:T(1,128)}, f32[1,256]{1,0:T(1,128)S(1)}, u32[]{:S(2)}) copy-start(f32[1,256]{1,0:T(1,128)S(1)} %get-tuple-element.386) | copy-start | bytes 3076
  66.3 1.5 %copy-start.13 = (f32[1,256]{1,0:T(1,128)}, f32[1,256]{1,0:T(1,128)S(1)}, u32[]{:S(2)}) copy-start(f32[1,256]{1,0:T(1,128)S(1)} %get-tuple-element.389) | copy-start | bytes 3076
  66.4 1.5 %copy-start.15 = (f32[1,256]{1,0:T(1,128)}, f32[1,256]{1,0:T(1,128)S(1)}, u32[]{:S(2)}) copy-start(f32[1,256]{1,0:T(1,128)S(1)} %get-tuple-element.392) | copy-start | bytes 3076
  66.4 1.4 %copy-start.17 = (f32[1,256]{1,0:T(1,128)}, f32[1,256]{1,0:T(1,128)S(1)}, u32[]{:S(2)}) copy-start(f32[1,256]{1,0:T(1,128)S(1)} %get-tuple-element.395) | copy-start | bytes 3076
  114.1 0.7 copy-start.31
  114.2 0.7 copy-start.34
  114.2 0.7 copy-start.35
  114.2 0.7 copy-start.36
  114.2 0.7 copy-start.42
  114.3 0.7 copy-start.43
  114.3 0.7 copy-start.44
  114.3 0.7 copy-start.48
  117.3 0.7 copy-start.59
  117.3 0.7 copy-start.63
  117.3 0.7 copy-start.64
  117.3 0.7 copy-start.65
  117.4 0.7 copy-start.66
  117.4 0.7 copy-start.67
  117.4 0.7 copy-start.68
  (40 other events, 26.7 us)
where the time goes:
time: 122 us
  blocking collectives  39.5 us (32%)
  local copies, waits for them, and re-layouts  34.9 us (29%)
  other arithmetic  31.8 us (26%)
  starting transfers between devices  6.31 us (5%)
  matrix products  3.9 us (3%)
  waiting for transfers between devices  3.33 us (3%)
  between operations  1.33 us (1%)
    psum x1, blocking collectives, body(): lax.psum((atm_part, ocean_late), ('sec', 'grp', 'blk'))  39.5 us
    gather x8, local copies, waits for them, and re-layouts, add_group(): chosen = jnp.take(tile_bank, tile_ids, axis=0)  22.7 us
    scatter-add x8, other arithmetic, add_group(): slot_sums.at[targets // ocean_blocks, :, targets % ocean_blocks]  15.4 us
    all_to_all x1, starting transfers between devices, body(): lax.all_to_all(outgoing, 'blk', split_axis=0, concat_axis=0, tiled=True)  6.31 us
    and x8, other arithmetic, add_group(): chosen = jnp.take(tile_bank, tile_ids, axis=0)  5.82 us
    gather x8, local copies, waits for them, and re-layouts, add_group(): picked = jnp.take(flux_blocks, sources, axis=1)  5.18 us
    dot_general x8, matrix products, add_group(): jnp.einsum('sgr,grc->gsc', picked, chosen, preferred_element_type=jnp.flo...  3.9 us
    all_to_all x1, waiting for transfers between devices, body(): lax.all_to_all(outgoing, 'blk', split_axis=0, concat_axis=0, tiled=True)  3.33 us
  transfers between devices with their start and end apart: 1, of which 1 were waited for; matrix products, arithmetic and copies ran while one was open for 4% of the time, Pallas kernels for 0%

commit v1 on v0

v1 whole, which is shorter than its diff:
```python
import functools

import jax
import jax.numpy as jnp
from jax import lax
from jax.experimental import pallas as pl
from jax.experimental.pallas import tpu as pltpu
from jax.sharding import PartitionSpec as P

MESH = pl.DeviceIdType.MESH


def up(value, unit):
    return -(-value // unit) * unit


def couple_kernel(
    blk_count,
    grp_count,
    side_count,
    ocean_blocks,
    scale,
    inverse_columns,
    count_ref,
    source_ref,
    tile_ref,
    target_ref,
    diffusivity_ref,
    depth_ref,
    flux_hbm,
    bank_hbm,
    tracers_hbm,
    mixed_hbm,
    response_ref,
    forced_ref,
    flux,
    bank,
    tracers,
    state,
    blocks,
    running,
    lists,
    lists_smem,
    outgoing,
    arrived,
    own_total,
    line_totals,
    line_sum,
    side_totals,
    couple,
    weight,
    carry,
    ratio,
    local_sem,
    send_sem,
    recv_sem,
    line_send,
    line_recv,
    side_send,
    side_recv,
):
    sec, grp, blk = lax.axis_index("sec"), lax.axis_index("grp"), lax.axis_index("blk")
    side = sec * grp_count + grp

    def line_peer(step):
        return lax.rem(blk + step, blk_count)

    def side_peer(step):
        return lax.rem(side + step, side_count)

    def line_id(peer):
        return (sec, grp, peer)

    def side_id(peer):
        return (peer // grp_count, lax.rem(peer, grp_count), blk)

    flux_copy = pltpu.make_async_copy(flux_hbm, flux, local_sem.at[0])
    bank_copy = pltpu.make_async_copy(bank_hbm, bank, local_sem.at[1])
    tracers_copy = pltpu.make_async_copy(tracers_hbm, tracers, local_sem.at[2])
    flux_copy.start()
    bank_copy.start()
    tracers_copy.start()

    barrier = pltpu.get_barrier_semaphore()

    @pl.loop(1, blk_count)
    def _(step):
        pl.semaphore_signal(barrier, inc=1, device_id=line_id(line_peer(step)), device_id_type=MESH)

    @pl.loop(1, side_count)
    def _(step):
        pl.semaphore_signal(barrier, inc=1, device_id=side_id(side_peer(step)), device_id_type=MESH)

    pairs = source_ref.shape[1]
    slots = lists.shape[1]
    live_count = count_ref[0]
    square = (pairs, pairs)
    row_at = lax.broadcasted_iota(jnp.int32, square, 0)
    lane_at = lax.broadcasted_iota(jnp.int32, square, 1)
    target_row = jnp.broadcast_to(target_ref[...], square)
    target_col = jnp.transpose(target_row)
    source_col = jnp.transpose(jnp.broadcast_to(source_ref[...], square))
    tile_col = jnp.transpose(jnp.broadcast_to(tile_ref[...], square))
    live_row = lane_at < live_count
    live_col = row_at < live_count
    hits = jnp.where((target_col == lane_at) & live_col, 1, 0)
    counts = jnp.sum(hits, axis=0, keepdims=True)
    padded = jnp.broadcast_to(lax.div(counts + 1, 2) * 2, square)
    before = jnp.where(lane_at < target_col, padded, 0)
    rank = jnp.where((target_row == target_col) & (lane_at < row_at) & live_row, 1, 0)
    slot = jnp.sum(before + rank, axis=1, keepdims=True)
    slot = jnp.where(live_col, jnp.broadcast_to(slot, square), slots)
    block_count = blocks.shape[0] - 1
    steps = running.shape[0] - 1
    lists[...] = jnp.zeros(lists.shape, jnp.int32)
    for first in range(0, slots, pairs):
        lanes = slice(first, first + pairs)
        chosen = slot == lane_at + first
        sources = jnp.sum(jnp.where(chosen, source_col - block_count, 0), axis=0, keepdims=True)
        tiles = jnp.sum(jnp.where(chosen, tile_col, 0), axis=0, keepdims=True)
        targets = jnp.sum(jnp.where(chosen, target_col + 1, 0), axis=0, keepdims=True)
        lists[0:1, lanes] = jnp.clip(sources + block_count, 0, block_count)
        lists[1:2, lanes] = jnp.clip(tiles, 0, bank.shape[0] - 1)
        lists[2:3, lanes] = targets
    upto = jnp.where(row_at <= lane_at, jnp.transpose(padded), 0)
    ends = lax.div(jnp.sum(upto, axis=0, keepdims=True), 2) - 1
    lists[8:9, 0:pairs] = jnp.where(counts > 0, jnp.clip(ends, 0, steps), steps)
    lists_copy = pltpu.make_async_copy(lists, lists_smem, local_sem.at[3])
    lists_copy.start()

    levels, columns = tracers.shape[0], tracers.shape[2]
    depth = depth_ref[...]
    level_at = lax.broadcasted_iota(jnp.int32, (levels, columns), 0)
    wet = jnp.where(level_at < depth, 1.0, 0.0)
    couple[0:1, :] = jnp.zeros((1, columns), jnp.float32)
    couple[1:levels, :] = diffusivity_ref[...] * wet[1:levels]
    couple[levels : levels + 1, :] = jnp.zeros((1, columns), jnp.float32)
    previous = jnp.zeros((1, columns), jnp.float32)
    forward = []
    for k in range(levels):
        a = couple[k : k + 1, :]
        b = couple[k + 1 : k + 2, :]
        inverse = 1.0 / (1.0 + a + b - a * previous)
        previous = b * inverse
        weight[k : k + 1, :] = jnp.where(depth > k, inverse, 0.0)
        carry[k : k + 1, :] = a * inverse
        ratio[k : k + 1, :] = previous
    for sweep in range(2):
        right = response_ref.at[0]
        unit = jnp.zeros((1, columns), jnp.float32)
        forward = []
        for k in range(levels):
            if sweep == 0:
                given = weight[0:1, :] if k == 0 else jnp.zeros((1, columns), jnp.float32)
            else:
                given = right[k : k + 1, :] * weight[k : k + 1, :]
            unit = given + carry[k : k + 1, :] * unit
            forward.append(unit)
        solved = forward[-1]
        response_ref[sweep, levels - 1 : levels, :] = solved
        for k in range(levels - 2, -1, -1):
            solved = forward[k] + ratio[k : k + 1, :] * solved
            response_ref[sweep, k : k + 1, :] = solved

    flux_copy.wait()
    subs, fields = flux.shape[0], flux.shape[1]
    width = blocks.shape[2]
    half = blocks.shape[1] // subs
    rows = blocks.shape[1]
    blocks[...] = jnp.zeros(blocks.shape, blocks.dtype)
    for b in range(block_count):
        for s in range(subs):
            blocks[b, s * half : s * half + fields, :] = flux[s, :, b * width : (b + 1) * width]
    running[steps] = jnp.zeros((rows, width), jnp.float32)
    spread = jnp.zeros((rows, width), jnp.float32)
    for b in range(block_count):
        spread = spread + blocks[b].astype(jnp.float32)
    own_total[...] = spread * scale

    lists_copy.wait()
    bank_copy.wait()

    def add_step(step, held):
        total, last = held
        first, second = 2 * step, 2 * step + 1
        target = lists_smem[2, first]
        left = jnp.concatenate([blocks[lists_smem[0, first]], blocks[lists_smem[0, second]]], axis=1)
        right = jnp.concatenate([bank[lists_smem[1, first]], bank[lists_smem[1, second]]], axis=0)
        keep = jnp.where(target == last, 1.0, 0.0).astype(jnp.float32)
        total = total * keep + jnp.dot(left, right, preferred_element_type=jnp.float32)
        running[step] = total
        return total, target

    lax.fori_loop(
        0, steps, add_step, (jnp.zeros((rows, width), jnp.float32), jnp.int32(-1)), unroll=4
    )

    @pl.loop(0, blk_count)
    def _(peer):
        spread = own_total[...]
        for o in range(ocean_blocks):
            out = running[lists_smem[8, peer * ocean_blocks + o]].astype(jnp.bfloat16)
            outgoing[peer, :, o * width : (o + 1) * width] = out
            spread = spread - out.astype(jnp.float32)
        own_total[...] = spread

    total_row = jnp.sum(jnp.transpose(own_total[...]), axis=0, keepdims=True)
    line_totals[blk] = jnp.broadcast_to(total_row, (8, rows))

    pl.semaphore_wait(barrier, blk_count - 1 + side_count - 1)

    def line_copy(peer, slot_at):
        return pltpu.make_async_remote_copy(
            src_ref=line_totals.at[blk],
            dst_ref=line_totals.at[slot_at],
            send_sem=line_send.at[peer],
            recv_sem=line_recv.at[slot_at],
            device_id=line_id(peer),
            device_id_type=MESH,
        )

    def data_copy(peer, slot_at):
        return pltpu.make_async_remote_copy(
            src_ref=outgoing.at[peer],
            dst_ref=arrived.at[slot_at],
            send_sem=send_sem.at[peer],
            recv_sem=recv_sem.at[slot_at],
            device_id=line_id(peer),
            device_id_type=MESH,
        )

    def side_copy(peer, slot_at):
        return pltpu.make_async_remote_copy(
            src_ref=line_sum,
            dst_ref=side_totals.at[slot_at],
            send_sem=side_send.at[peer],
            recv_sem=side_recv.at[slot_at],
            device_id=side_id(peer),
            device_id_type=MESH,
        )

    @pl.loop(1, blk_count)
    def _(step):
        line_copy(line_peer(step), blk).start()

    @pl.loop(1, blk_count)
    def _(step):
        data_copy(line_peer(step), blk).start()

    tracers_copy.wait()

    def forward_level(source):
        def level(k, held):
            held = source[k].astype(jnp.float32) * weight[pl.ds(k, 1), :] + carry[pl.ds(k, 1), :] * held
            state[k] = held
            return held

        return level

    def back_level(i, held):
        k = levels - 2 - i
        held = state[k] + ratio[pl.ds(k, 1), :] * held
        state[k] = held
        return held

    nothing = jnp.zeros((fields, columns), jnp.float32)
    bottom = lax.fori_loop(0, levels, forward_level(tracers), nothing)

    @pl.loop(1, blk_count)
    def _(step):
        peer = line_peer(step)
        line_copy(peer, peer).wait_recv()

    summed = line_totals[0]
    for p in range(1, blk_count):
        summed = summed + line_totals[p]
    line_sum[...] = summed

    @pl.loop(1, side_count)
    def _(step):
        side_copy(side_peer(step), side).start()

    lax.fori_loop(0, levels - 1, back_level, bottom)
    bottom = lax.fori_loop(0, levels, forward_level(state), nothing)
    lax.fori_loop(0, levels - 1, back_level, bottom)
    mixed_copy = pltpu.make_async_copy(state, mixed_hbm, local_sem.at[4])
    mixed_copy.start()

    @pl.loop(1, side_count)
    def _(step):
        peer = side_peer(step)
        side_copy(peer, peer).wait_recv()

    side_totals[side] = line_sum[...]
    everything = side_totals[0]
    for p in range(1, side_count):
        everything = everything + side_totals[p]
    correction = jnp.transpose(jnp.broadcast_to(everything[0:1, :] * inverse_columns, (rows, rows)))

    @pl.loop(1, blk_count)
    def _(step):
        peer = line_peer(step)
        data_copy(peer, peer).wait_recv()

    arrived[blk] = outgoing[blk]
    for o in range(ocean_blocks):
        lanes = slice(o * width, (o + 1) * width)
        forced = arrived[0, :, lanes].astype(jnp.float32)
        for p in range(1, blk_count):
            forced = forced + arrived[p, :, lanes].astype(jnp.float32)
        forced_ref[:, lanes] = forced + correction

    mixed_copy.wait()

    @pl.loop(1, blk_count)
    def _(step):
        peer = line_peer(step)
        line_copy(peer, blk).wait_send()
        data_copy(peer, blk).wait_send()

    @pl.loop(1, side_count)
    def _(step):
        side_copy(side_peer(step), side).wait_send()


def body(
    atm_flux,
    tile_bank,
    pair_count,
    pair_source,
    pair_tile,
    pair_target,
    tracers,
    diffusivity,
    column_depth,
):
    subs, fields, atm_rows = atm_flux.shape
    width = tile_bank.shape[1]
    block_count = atm_rows // width
    levels, _, columns = tracers.shape
    ocean_blocks = columns // width
    blk_count, grp_count = lax.axis_size("blk"), lax.axis_size("grp")
    side_count = lax.axis_size("sec") * grp_count
    pairs = pair_source.shape[0]
    half = up(fields, 64)
    rows = subs * half
    slot_count = up(pairs + blk_count * ocean_blocks, 2)
    steps = slot_count // 2
    steps_up = up(steps, 4)
    slots = up(2 * steps_up, 128)
    f32, bf16 = jnp.float32, jnp.bfloat16
    vmem = pl.BlockSpec(memory_space=pltpu.VMEM)
    smem = pl.BlockSpec(memory_space=pltpu.SMEM)
    anywhere = pl.BlockSpec(memory_space=pl.ANY)
    mixed, response, forced = pl.pallas_call(
        functools.partial(
            couple_kernel,
            blk_count,
            grp_count,
            side_count,
            ocean_blocks,
            ocean_blocks / block_count,
            1.0 / (columns * blk_count * side_count),
        ),
        out_shape=(
            jax.ShapeDtypeStruct((levels, fields, columns), f32),
            jax.ShapeDtypeStruct((2, levels, columns), f32),
            jax.ShapeDtypeStruct((rows, columns), f32),
        ),
        in_specs=[smem, vmem, vmem, vmem, vmem, vmem, anywhere, anywhere, anywhere],
        out_specs=(anywhere, vmem, vmem),
        scratch_shapes=[
            pltpu.VMEM(atm_flux.shape, bf16),
            pltpu.VMEM(tile_bank.shape, bf16),
            pltpu.VMEM(tracers.shape, bf16),
            pltpu.VMEM(tracers.shape, f32),
            pltpu.VMEM((block_count + 1, rows, width), bf16),
            pltpu.VMEM((steps_up + 1, rows, width), f32),
            pltpu.VMEM((16, slots), jnp.int32),
            pltpu.SMEM((16, slots), jnp.int32),
            pltpu.VMEM((blk_count, rows, columns), bf16),
            pltpu.VMEM((blk_count, rows, columns), bf16),
            pltpu.VMEM((rows, width), f32),
            pltpu.VMEM((blk_count, 8, rows), f32),
            pltpu.VMEM((8, rows), f32),
            pltpu.VMEM((side_count, 8, rows), f32),
            pltpu.VMEM((levels + 8, columns), f32),
            pltpu.VMEM((levels, columns), f32),
            pltpu.VMEM((levels, columns), f32),
            pltpu.VMEM((levels, columns), f32),
            pltpu.SemaphoreType.DMA((5,)),
            pltpu.SemaphoreType.DMA((blk_count,)),
            pltpu.SemaphoreType.DMA((blk_count,)),
            pltpu.SemaphoreType.DMA((blk_count,)),
            pltpu.SemaphoreType.DMA((blk_count,)),
            pltpu.SemaphoreType.DMA((side_count,)),
            pltpu.SemaphoreType.DMA((side_count,)),
        ],
        compiler_params=pltpu.CompilerParams(
            collective_id=0, has_side_effects=True, vmem_limit_bytes=48 * 1024 * 1024
        ),
    )(
        pair_count,
        pair_source.reshape(1, pairs),
        pair_tile.reshape(1, pairs),
        pair_target.reshape(1, pairs),
        diffusivity,
        column_depth.reshape(1, columns),
        atm_flux,
        tile_bank,
        tracers,
    )
    forced = forced.reshape(subs, half, columns)[:, :fields]
    return (
        mixed
        + response[1][:, None, :] * forced[0][None]
        + response[0][:, None, :] * forced[1][None]
    )


def solution(mesh):
    over = ("sec", "grp", "blk")
    placed = (
        P(None, None, over),
        P(),
        P(over),
        P(over),
        P(over),
        P(over),
        P(None, None, over),
        P(None, over),
        P(over),
    )
    return jax.shard_map(
        body, mesh=mesh, in_specs=placed, out_specs=P(None, None, over), check_vma=False
    )
```

time: 122 us -> 24.5 us (0.20)
  blocking collectives: 39.5 us -> 0 us
  other arithmetic: 31.8 us -> 0.33 us
  local copies, waits for them, and re-layouts: 34.9 us -> 5.38 us
  Pallas kernels: 0 us -> 17.8 us
  starting transfers between devices: 6.31 us -> 0 us
  matrix products: 3.9 us -> 0 us
  waiting for transfers between devices: 3.33 us -> 0 us
    psum x1 -> x0, blocking collectives: 39.5 us -> none  [body(): lax.psum((atm_part, ocean_late), ('sec', 'grp', 'blk'))]
    gather x16 -> x0, local copies, waits for them, and re-layouts: 27.9 us -> none  [the longest x8 22.7 us: add_group(): chosen = jnp.take(tile_bank, tile_ids, axis=0)]
    pallas_call x0 -> x1, Pallas kernels: none -> 17.8 us  [body(): pl.pallas_call(functools.partial(couple_kernel, blk_count, grp_count, sid...]
    scatter-add x10 -> x0, other arithmetic: 16.2 us -> none  [the longest x8 15.4 us: add_group(): slot_sums.at[targets // ocean_blocks, :, targets % ocean_blocks]]
    and x16 -> x0, other arithmetic: 6.45 us -> none  [the longest x8 5.82 us: add_group(): chosen = jnp.take(tile_bank, tile_ids, axis=0)]
    all_to_all x1 -> x0, starting transfers between devices: 6.31 us -> none  [body(): lax.all_to_all(outgoing, 'blk', split_axis=0, concat_axis=0, tiled=True)]
    dot_general x8 -> x0, matrix products: 3.9 us -> none  [add_group(): jnp.einsum('sgr,grc->gsc', picked, chosen, preferred_element_type=jnp.flo...]
    all_to_all x1 -> x0, waiting for transfers between devices: 3.33 us -> none  [body(): lax.all_to_all(outgoing, 'blk', split_axis=0, concat_axis=0, tiled=True)]
  transfers between devices with their start and end apart: 1 -> 0, of which waited for: 1 -> 0; matrix products, arithmetic and copies ran while one was open for 4% -> 0% of each run, Pallas kernels for 0% -> 0%
where the time goes in v1:
time: 24.5 us; the launch traced here: 24.3 us
  Pallas kernels  17.8 us (73%)
  local copies, waits for them, and re-layouts  5.38 us (22%)
  between operations  0.8 us (3%)
  other arithmetic  0.33 us (1%)
    pallas_call x1, Pallas kernels, body(): pl.pallas_call(functools.partial(couple_kernel, blk_count, grp_count, sid...  17.8 us
    unnamed x12, local copies, waits for them, and re-layouts  2.95 us
    add x1, local copies, waits for them, and re-layouts, body(): mixed + response[1][:, None, :] * forced[0][None]  2.41 us

profile of v1, /device:TPU:0, one launch (start us, length us, event | category | flops | bytes accessed | tf_op | source)
XLA Modules:
  0.0 24.3 jit_solution(14270235754456346565)
XLA Ops:
  0.0 0.0 copy-start.1
  0.0 0.0 copy-start
  0.0 0.0 copy-start.4
  0.0 0.0 copy-start.3
  0.0 0.0 copy-start.2
  0.7 1.2 %copy.10.flux_hbm = bf16[2,60,2048]{2,1,0:T(8,128)(2,1)S(1)} copy(bf16[2,60,2048]{2,0,1:T(2,128)(2,1)} %param.9) | data formatting | bytes 983040 | tf_op args[0]
  1.9 1.8 %copy.11.tracers_hbm = bf16[32,60,256]{2,1,0:T(8,128)(2,1)S(1)} copy(bf16[32,60,256]{2,0,1:T(8,128)(2,1)} %param.15) | data formatting | bytes 1966080 | tf_op args[6]
  3.7 0.0 copy-done.1
  3.7 0.0 copy-done
  3.7 0.0 copy-done.4
  3.7 0.0 copy-done.3
  3.7 0.0 copy-done.2
  3.7 17.8 %shard_map.91 = (f32[32,60,256]{2,1,0:T(8,128)S(1)}, f32[2,32,256]{2,1,0:T(8,128)S(1)}, f32[128,256]{1,0:T(8,128)S(1)}) custom-call(s32[1]{0:T(128)S(6)} %copy.13.count_ref, s32[1,128]{1,0:T(1,128)S(1)} %bitcast.15, s32[1,128]{1,0:T(1,128)S(1)} %bitcast.16, s32[1,128]{1,0:T(1,128)S(1)} %bitcast.17, f32[31,256]{1,0:T(8,128)S(1)} %copy-done, ...), custom_call_target="tpu_custom_call" | custom-call | tf_op jit(solution)/shard_map/pallas_call | solution.py:355
  21.5 0.3 %multiply_add_fusion = f32[32,60,256]{2,1,0:T(8,128)S(1)} fusion(f32[32,60,256]{2,1,0:T(8,128)S(1)} %get-tuple-element.8, f32[60,256]{1,0:T(8,128)S(1)} %get-tuple-element.12, f32[32,256]{1,0:T(8,128)S(1)} %get-tuple-element.14, f32[60,256]{1,0:T(8,128)S(1)} %get-tuple-element.11, f32[32,256]{1,0:T(8,128)S(1)} %get-tuple-element.13), kind=kLoop, calls=%fused_computation | loop fusion | flops 1966080 | bytes 4120576 | tf_op jit(solution)/shard_map/add | solution.py:415
  21.9 2.4 %copy.12 = f32[32,60,256]{2,0,1:T(8,128)} copy(f32[32,60,256]{2,1,0:T(8,128)S(1)} %multiply_add_fusion) | data formatting | bytes 3932160 | tf_op jit(solution)/shard_map/add | solution.py:415
  (2 shorter events, 0.0 us)
Async XLA Ops:
  0.0 3.7 %copy-start.1 = (s32[256]{0:T(256)S(1)}, s32[256]{0:T(256)}, u32[]{:S(2)}) copy-start(s32[256]{0:T(256)} %param.17) | copy-start | bytes 3076
  0.0 3.7 %copy-start = (f32[31,256]{1,0:T(8,128)S(1)}, f32[31,256]{1,0:T(8,128)}, u32[]{:S(2)}) copy-start(f32[31,256]{1,0:T(8,128)} %diffusivity_ref.1) | copy-start | bytes 95236
  0.0 3.7 %copy-start.4 = (s32[128]{0:T(128)S(1)}, s32[128]{0:T(128)}, u32[]{:S(2)}) copy-start(s32[128]{0:T(128)} %param.14) | copy-start | bytes 1540
  0.0 3.7 %copy-start.3 = (s32[128]{0:T(128)S(1)}, s32[128]{0:T(128)}, u32[]{:S(2)}) copy-start(s32[128]{0:T(128)} %param.13) | copy-start | bytes 1540
  0.0 3.7 %copy-start.2 = (s32[128]{0:T(128)S(1)}, s32[128]{0:T(128)}, u32[]{:S(2)}) copy-start(s32[128]{0:T(128)} %param.12) | copy-start | bytes 1540

commit v2 on v1

--- a/solution.py
+++ b/solution.py
@@ -30,13 +30,15 @@
     flux_hbm,
     bank_hbm,
     tracers_hbm,
-    mixed_hbm,
+    mixed_ref,
     response_ref,
     forced_ref,
     flux,
     bank,
     tracers,
+    given,
     state,
+    forced_rows,
     blocks,
     running,
     lists,
@@ -128,7 +130,90 @@
     lists_copy = pltpu.make_async_copy(lists, lists_smem, local_sem.at[3])
     lists_copy.start()
 
-    levels, columns = tracers.shape[0], tracers.shape[2]
+    flux_copy.wait()
+    fields, subs = flux.shape[0], flux.shape[1]
+    rows, width = blocks.shape[1], blocks.shape[2]
+    stack = fields * subs
+    blocks[...] = jnp.zeros(blocks.shape, blocks.dtype)
+    for b in range(block_count):
+        blocks[b, 0:stack, :] = flux[:, :, b * width : (b + 1) * width].reshape(stack, width)
+    running[steps] = jnp.zeros((rows, width), jnp.float32)
+    spread = jnp.zeros((rows, width), jnp.float32)
+    for b in range(block_count):
+        spread = spread + blocks[b].astype(jnp.float32)
+    own_total[...] = spread * scale
+
+    lists_copy.wait()
+    bank_copy.wait()
+
+    def add_step(step, held):
+        total, last = held
+        first, second = 2 * step, 2 * step + 1
+        target = lists_smem[2, first]
+        left = jnp.concatenate([blocks[lists_smem[0, first]], blocks[lists_smem[0, second]]], axis=1)
+        right = jnp.concatenate([bank[lists_smem[1, first]], bank[lists_smem[1, second]]], axis=0)
+        keep = jnp.where(target == last, 1.0, 0.0).astype(jnp.float32)
+        total = total * keep + jnp.dot(left, right, preferred_element_type=jnp.float32)
+        running[step] = total
+        return total, target
+
+    lax.fori_loop(
+        0, steps, add_step, (jnp.zeros((rows, width), jnp.float32), jnp.int32(-1)), unroll=4
+    )
+
+    @pl.loop(0, blk_count)
+    def _(peer):
+        spread = own_total[...]
+        for o in range(ocean_blocks):
+            out = running[lists_smem[8, peer * ocean_blocks + o]].astype(jnp.bfloat16)
+            outgoing[peer, :, o * width : (o + 1) * width] = out
+            spread = spread - out.astype(jnp.float32)
+        own_total[...] = spread
+
+    total_row = jnp.sum(jnp.transpose(own_total[...]), axis=0, keepdims=True)
+    line_totals[blk] = jnp.broadcast_to(total_row, (8, rows))
+
+    pl.semaphore_wait(barrier, blk_count - 1 + side_count - 1)
+
+    def line_copy(peer, slot_at):
+        return pltpu.make_async_remote_copy(
+            src_ref=line_totals.at[blk],
+            dst_ref=line_totals.at[slot_at],
+            send_sem=line_send.at[peer],
+            recv_sem=line_recv.at[slot_at],
+            device_id=line_id(peer),
+            device_id_type=MESH,
+        )
+
+    def data_copy(peer, slot_at):
+        return pltpu.make_async_remote_copy(
+            src_ref=outgoing.at[peer],
+            dst_ref=arrived.at[slot_at],
+            send_sem=send_sem.at[peer],
+            recv_sem=recv_sem.at[slot_at],
+            device_id=line_id(peer),
+            device_id_type=MESH,
+        )
+
+    def side_copy(peer, slot_at):
+        return pltpu.make_async_remote_copy(
+            src_ref=line_sum,
+            dst_ref=side_totals.at[slot_at],
+            send_sem=side_send.at[peer],
+            recv_sem=side_recv.at[slot_at],
+            device_id=side_id(peer),
+            device_id_type=MESH,
+        )
+
+    @pl.loop(1, blk_count)
+    def _(step):
+        line_copy(line_peer(step), blk).start()
+
+    @pl.loop(1, blk_count)
+    def _(step):
+        data_copy(line_peer(step), blk).start()
+
+    fields, levels, columns = tracers.shape
     depth = depth_ref[...]
     level_at = lax.broadcasted_iota(jnp.int32, (levels, columns), 0)
     wet = jnp.where(level_at < depth, 1.0, 0.0)
@@ -136,7 +221,6 @@
     couple[1:levels, :] = diffusivity_ref[...] * wet[1:levels]
     couple[levels : levels + 1, :] = jnp.zeros((1, columns), jnp.float32)
     previous = jnp.zeros((1, columns), jnp.float32)
-    forward = []
     for k in range(levels):
         a = couple[k : k + 1, :]
         b = couple[k + 1 : k + 2, :]
@@ -151,10 +235,10 @@
         forward = []
         for k in range(levels):
             if sweep == 0:
-                given = weight[0:1, :] if k == 0 else jnp.zeros((1, columns), jnp.float32)
+                pushed = weight[0:1, :] if k == 0 else jnp.zeros((1, columns), jnp.float32)
             else:
-                given = right[k : k + 1, :] * weight[k : k + 1, :]
-            unit = given + carry[k : k + 1, :] * unit
+                pushed = right[k : k + 1, :] * weight[k : k + 1, :]
+            unit = pushed + carry[k : k + 1, :] * unit
             forward.append(unit)
         solved = forward[-1]
         response_ref[sweep, levels - 1 : levels, :] = solved
@@ -162,100 +246,32 @@
             solved = forward[k] + ratio[k : k + 1, :] * solved
             response_ref[sweep, k : k + 1, :] = solved
 
-    flux_copy.wait()
-    subs, fields = flux.shape[0], flux.shape[1]
-    width = blocks.shape[2]
-    half = blocks.shape[1] // subs
-    rows = blocks.shape[1]
-    blocks[...] = jnp.zeros(blocks.shape, blocks.dtype)
-    for b in range(block_count):
-        for s in range(subs):
-            blocks[b, s * half : s * half + fields, :] = flux[s, :, b * width : (b + 1) * width]
-    running[steps] = jnp.zeros((rows, width), jnp.float32)
-    spread = jnp.zeros((rows, width), jnp.float32)
-    for b in range(block_count):
-        spread = spread + blocks[b].astype(jnp.float32)
-    own_total[...] = spread * scale
-
-    lists_copy.wait()
-    bank_copy.wait()
-
-    def add_step(step, held):
-        total, last = held
-        first, second = 2 * step, 2 * step + 1
-        target = lists_smem[2, first]
-        left = jnp.concatenate([blocks[lists_smem[0, first]], blocks[lists_smem[0, second]]], axis=1)
-        right = jnp.concatenate([bank[lists_smem[1, first]], bank[lists_smem[1, second]]], axis=0)
-        keep = jnp.where(target == last, 1.0, 0.0).astype(jnp.float32)
-        total = total * keep + jnp.dot(left, right, preferred_element_type=jnp.float32)
-        running[step] = total
-        return total, target
-
-    lax.fori_loop(
-        0, steps, add_step, (jnp.zeros((rows, width), jnp.float32), jnp.int32(-1)), unroll=4
-    )
-
-    @pl.loop(0, blk_count)
-    def _(peer):
-        spread = own_total[...]
+    tracers_copy.wait()
+
+    @pl.loop(0, fields)
+    def _(f):
+        at = pl.ds(pl.multiple_of(f * levels, levels), levels)
         for o in range(ocean_blocks):
-            out = running[lists_smem[8, peer * ocean_blocks + o]].astype(jnp.bfloat16)
-            outgoing[peer, :, o * width : (o + 1) * width] = out
-            spread = spread - out.astype(jnp.float32)
-        own_total[...] = spread
-
-    total_row = jnp.sum(jnp.transpose(own_total[...]), axis=0, keepdims=True)
-    line_totals[blk] = jnp.broadcast_to(total_row, (8, rows))
-
-    pl.semaphore_wait(barrier, blk_count - 1 + side_count - 1)
-
-    def line_copy(peer, slot_at):
-        return pltpu.make_async_remote_copy(
-            src_ref=line_totals.at[blk],
-            dst_ref=line_totals.at[slot_at],
-            send_sem=line_send.at[peer],
-            recv_sem=line_recv.at[slot_at],
-            device_id=line_id(peer),
-            device_id_type=MESH,
-        )
-
-    def data_copy(peer, slot_at):
-        return pltpu.make_async_remote_copy(
-            src_ref=outgoing.at[peer],
-            dst_ref=arrived.at[slot_at],
-            send_sem=send_sem.at[peer],
-            recv_sem=recv_sem.at[slot_at],
-            device_id=line_id(peer),
-            device_id_type=MESH,
-        )
-
-    def side_copy(peer, slot_at):
-        return pltpu.make_async_remote_copy(
-            src_ref=line_sum,
-            dst_ref=side_totals.at[slot_at],
-            send_sem=side_send.at[peer],
-            recv_sem=side_recv.at[slot_at],
-            device_id=side_id(peer),
-            device_id_type=MESH,
-        )
-
-    @pl.loop(1, blk_count)
-    def _(step):
-        line_copy(line_peer(step), blk).start()
-
-    @pl.loop(1, blk_count)
-    def _(step):
-        data_copy(line_peer(step), blk).start()
-
-    tracers_copy.wait()
-
-    def forward_level(source):
-        def level(k, held):
-            held = source[k].astype(jnp.float32) * weight[pl.ds(k, 1), :] + carry[pl.ds(k, 1), :] * held
-            state[k] = held
-            return held
-
-        return level
+            lanes = slice(o * width, (o + 1) * width)
+            given[o, at, :] = tracers[f, :, lanes].astype(jnp.float32)
+
+    def level_rows(k):
+        return pl.ds(k, fields, stride=levels)
+
+    def put_level(k, held):
+        for o in range(ocean_blocks):
+            mixed_ref[o, level_rows(k), :] = held[:, o * width : (o + 1) * width]
+
+    def first_level(k, held):
+        read = [given[o, level_rows(k), :] for o in range(ocean_blocks)]
+        held = jnp.concatenate(read, axis=1) * weight[pl.ds(k, 1), :] + carry[pl.ds(k, 1), :] * held
+        state[k] = held
+        return held
+
+    def forward_level(k, held):
+        held = state[k] * weight[pl.ds(k, 1), :] + carry[pl.ds(k, 1), :] * held
+        state[k] = held
+        return held
 
     def back_level(i, held):
         k = levels - 2 - i
@@ -263,8 +279,14 @@
         state[k] = held
         return held
 
+    def last_level(i, held):
+        k = levels - 2 - i
+        held = state[k] + ratio[pl.ds(k, 1), :] * held
+        put_level(k, held)
+        return held
+
     nothing = jnp.zeros((fields, columns), jnp.float32)
-    bottom = lax.fori_loop(0, levels, forward_level(tracers), nothing)
+    bottom = lax.fori_loop(0, levels, first_level, nothing, unroll=4)
 
     @pl.loop(1, blk_count)
     def _(step):
@@ -281,10 +303,9 @@
         side_copy(side_peer(step), side).start()
 
     lax.fori_loop(0, levels - 1, back_level, bottom)
-    bottom = lax.fori_loop(0, levels, forward_level(state), nothing)
-    lax.fori_loop(0, levels - 1, back_level, bottom)
-    mixed_copy = pltpu.make_async_copy(state, mixed_hbm, local_sem.at[4])
-    mixed_copy.start()
+    bottom = lax.fori_loop(0, levels, forward_level, nothing, unroll=4)
+    put_level(levels - 1, bottom)
+    lax.fori_loop(0, levels - 1, last_level, bottom)
 
     @pl.loop(1, side_count)
     def _(step):
@@ -308,9 +329,9 @@
         forced = arrived[0, :, lanes].astype(jnp.float32)
         for p in range(1, blk_count):
             forced = forced + arrived[p, :, lanes].astype(jnp.float32)
-        forced_ref[:, lanes] = forced + correction
-
-    mixed_copy.wait()
+        forced_rows[o] = forced + correction
+        for s in range(subs):
+            forced_ref[s, :, lanes] = forced_rows[o, pl.ds(s, fields, stride=subs), :]
 
     @pl.loop(1, blk_count)
     def _(step):
@@ -321,6 +342,31 @@
     @pl.loop(1, side_count)
     def _(step):
         side_copy(side_peer(step), side).wait_send()
+
+
+def join_kernel(parts, mixed_ref, response_ref, forced_ref, result_hbm, result, sems):
+    fields, levels, columns = result.shape
+    halves, _, width = mixed_ref.shape
+    near, far = response_ref[0], response_ref[1]
+    part = fields // parts
+
+    def copy(n):
+        at = pl.ds(n * part, part)
+        return pltpu.make_async_copy(result.at[at], result_hbm.at[at], sems.at[n])
+
+    for n in range(parts):
+
+        @pl.loop(n * part, (n + 1) * part)
+        def _(f):
+            at = pl.ds(pl.multiple_of(f * levels, levels), levels)
+            mixed = jnp.concatenate([mixed_ref[o, at, :] for o in range(halves)], axis=1)
+            early = forced_ref[0, pl.ds(f, 1), :]
+            late = forced_ref[1, pl.ds(f, 1), :]
+            result[f] = mixed + far * early + near * late
+
+        copy(n).start()
+    for n in range(parts):
+        copy(n).wait()
 
 
 def body(
@@ -342,8 +388,7 @@
     blk_count, grp_count = lax.axis_size("blk"), lax.axis_size("grp")
     side_count = lax.axis_size("sec") * grp_count
     pairs = pair_source.shape[0]
-    half = up(fields, 64)
-    rows = subs * half
+    rows = up(subs * fields, 128)
     slot_count = up(pairs + blk_count * ocean_blocks, 2)
     steps = slot_count // 2
     steps_up = up(steps, 4)
@@ -363,17 +408,19 @@
             1.0 / (columns * blk_count * side_count),
         ),
         out_shape=(
-            jax.ShapeDtypeStruct((levels, fields, columns), f32),
+            jax.ShapeDtypeStruct((ocean_blocks, fields * levels, width), f32),
             jax.ShapeDtypeStruct((2, levels, columns), f32),
-            jax.ShapeDtypeStruct((rows, columns), f32),
+            jax.ShapeDtypeStruct((subs, fields, columns), f32),
         ),
         in_specs=[smem, vmem, vmem, vmem, vmem, vmem, anywhere, anywhere, anywhere],
-        out_specs=(anywhere, vmem, vmem),
+        out_specs=(vmem, vmem, vmem),
         scratch_shapes=[
-            pltpu.VMEM(atm_flux.shape, bf16),
+            pltpu.VMEM((fields, subs, atm_rows), bf16),
             pltpu.VMEM(tile_bank.shape, bf16),
-            pltpu.VMEM(tracers.shape, bf16),
-            pltpu.VMEM(tracers.shape, f32),
+            pltpu.VMEM((fields, levels, columns), bf16),
+            pltpu.VMEM((ocean_blocks, fields * levels, width), f32),
+            pltpu.VMEM((levels, fields, columns), f32),
+            pltpu.VMEM((ocean_blocks, rows, width), f32),
             pltpu.VMEM((block_count + 1, rows, width), bf16),
             pltpu.VMEM((steps_up + 1, rows, width), f32),
             pltpu.VMEM((16, slots), jnp.int32),
@@ -406,16 +453,23 @@
         pair_target.reshape(1, pairs),
         diffusivity,
         column_depth.reshape(1, columns),
-        atm_flux,
+        jnp.transpose(atm_flux, (1, 0, 2)),
         tile_bank,
-        tracers,
+        jnp.transpose(tracers, (1, 0, 2)),
     )
-    forced = forced.reshape(subs, half, columns)[:, :fields]
-    return (
-        mixed
-        + response[1][:, None, :] * forced[0][None]
-        + response[0][:, None, :] * forced[1][None]
-    )
+    parts = 4 if fields % 4 == 0 else 1
+    result = pl.pallas_call(
+        functools.partial(join_kernel, parts),
+        out_shape=jax.ShapeDtypeStruct((fields, levels, columns), f32),
+        in_specs=[vmem, vmem, vmem],
+        out_specs=anywhere,
+        scratch_shapes=[
+            pltpu.VMEM((fields, levels, columns), f32),
+            pltpu.SemaphoreType.DMA((parts,)),
+        ],
+        compiler_params=pltpu.CompilerParams(vmem_limit_bytes=16 * 1024 * 1024),
+    )(mixed, response, forced)
+    return jnp.transpose(result, (1, 0, 2))
 
 
 def solution(mesh):

time: 24.5 us -> 26.1 us (1.065)
  Pallas kernels: 17.8 us -> 19.5 us
  other arithmetic: 0.33 us -> 0 us
    unnamed x12 -> x14, local copies, waits for them, and re-layouts: 2.95 us -> 5.62 us
    add x1 -> x0, local copies, waits for them, and re-layouts: 2.41 us -> none  [body(): mixed + response[1][:, None, :] * forced[0][None]]
    pallas_call x0 -> x1, Pallas kernels: none -> 1.46 us  [body(): pl.pallas_call(functools.partial(join_kernel, parts), out_shape=jax.Shape...]
    add x1 -> x0, other arithmetic: 0.33 us -> none  [body(): mixed + response[1][:, None, :] * forced[0][None]]
where the time goes in v2:
time: 26.1 us; the launch traced here: 25.8 us
  Pallas kernels  19.5 us (75%)
  local copies, waits for them, and re-layouts  5.62 us (22%)
  between operations  0.67 us (3%)
    pallas_call x1, Pallas kernels, body(): pl.pallas_call(functools.partial(couple_kernel, blk_count, grp_count, sid...  18 us
    unnamed x14, local copies, waits for them, and re-layouts  5.62 us
    pallas_call x1, Pallas kernels, body(): pl.pallas_call(functools.partial(join_kernel, parts), out_shape=jax.Shape...  1.46 us

profile of v2, /device:TPU:0, one launch (start us, length us, event | category | flops | bytes accessed | tf_op | source)
XLA Modules:
  0.0 25.8 jit_solution(6475033271523240220)
XLA Ops:
  0.7 0.0 copy-start
  0.7 1.2 %copy-done = bf16[32,60,256]{2,0,1:T(8,128)(2,1)S(1)} copy-done((bf16[32,60,256]{2,0,1:T(8,128)(2,1)S(1)}, bf16[32,60,256]{2,0,1:T(8,128)(2,1)}, u32[]{:S(2)}) %copy-start) | copy-done | bytes 983064
  1.9 0.0 copy-start.1
  1.9 1.0 %copy-done.1 = bf16[2,60,2048]{2,0,1:T(2,128)(2,1)S(1)} copy-done((bf16[2,60,2048]{2,0,1:T(2,128)(2,1)S(1)}, bf16[2,60,2048]{2,0,1:T(2,128)(2,1)}, u32[]{:S(2)}) %copy-start.1) | copy-done | bytes 491544
  2.9 0.0 copy-start.2
  2.9 0.8 %copy-done.2 = f32[31,256]{1,0:T(8,128)S(1)} copy-done((f32[31,256]{1,0:T(8,128)S(1)}, f32[31,256]{1,0:T(8,128)}, u32[]{:S(2)}) %copy-start.2) | copy-done | bytes 31768
  3.6 0.0 copy-start.3
  3.6 0.7 %copy-done.3 = s32[256]{0:T(256)S(1)} copy-done((s32[256]{0:T(256)S(1)}, s32[256]{0:T(256)}, u32[]{:S(2)}) %copy-start.3) | copy-done | bytes 1048
  4.3 0.0 copy-start.4
  4.3 0.7 %copy-done.4 = s32[128]{0:T(128)S(1)} copy-done((s32[128]{0:T(128)S(1)}, s32[128]{0:T(128)}, u32[]{:S(2)}) %copy-start.4) | copy-done | bytes 536
  5.0 0.0 copy-start.5
  5.0 0.7 %copy-done.5 = s32[128]{0:T(128)S(1)} copy-done((s32[128]{0:T(128)S(1)}, s32[128]{0:T(128)}, u32[]{:S(2)}) %copy-start.5) | copy-done | bytes 536
  5.6 0.0 copy-start.6
  5.6 0.7 %copy-done.6 = s32[128]{0:T(128)S(1)} copy-done((s32[128]{0:T(128)S(1)}, s32[128]{0:T(128)}, u32[]{:S(2)}) %copy-start.6) | copy-done | bytes 536
  6.3 18.0 %shard_map.91 = (f32[2,1920,128]{2,1,0:T(8,128)S(1)}, f32[2,32,256]{2,1,0:T(8,128)S(1)}, f32[2,60,256]{2,1,0:T(8,128)S(1)}) custom-call(s32[1]{0:T(128)S(6)} %copy.10.count_ref, s32[1,128]{1,0:T(1,128)S(1)} %bitcast.10, s32[1,128]{1,0:T(1,128)S(1)} %bitcast.11, s32[1,128]{1,0:T(1,128)S(1)} %bitcast.12, f32[31,256]{1,0:T(8,128)S(1)} %copy-done.2, ...), custom_call_target="tpu_custom_call" | custom-call | tf_op jit(solution)/shard_map/pallas_call | solution.py:400
  24.3 1.5 %shard_map.92 = f32[60,32,256]{2,1,0:T(8,128)} custom-call(f32[2,1920,128]{2,1,0:T(8,128)S(1)} %get-tuple-element.8.mixed_ref, f32[2,32,256]{2,1,0:T(8,128)S(1)} %get-tuple-element.9.response_ref, f32[2,60,256]{2,1,0:T(8,128)S(1)} %get-tuple-element.10.forced_ref), custom_call_target="tpu_custom_call" | custom-call | tf_op jit(solution)/shard_map/pallas_call | solution.py:461
Async XLA Ops:
  0.7 1.2 %copy-start = (bf16[32,60,256]{2,0,1:T(8,128)(2,1)S(1)}, bf16[32,60,256]{2,0,1:T(8,128)(2,1)}, u32[]{:S(2)}) copy-start(bf16[32,60,256]{2,0,1:T(8,128)(2,1)} %param.15) | copy-start | bytes 2949124
  1.9 1.0 %copy-start.1 = (bf16[2,60,2048]{2,0,1:T(2,128)(2,1)S(1)}, bf16[2,60,2048]{2,0,1:T(2,128)(2,1)}, u32[]{:S(2)}) copy-start(bf16[2,60,2048]{2,0,1:T(2,128)(2,1)} %param.9) | copy-start | bytes 1474564
  2.9 0.8 %copy-start.2 = (f32[31,256]{1,0:T(8,128)S(1)}, f32[31,256]{1,0:T(8,128)}, u32[]{:S(2)}) copy-start(f32[31,256]{1,0:T(8,128)} %diffusivity_ref.1) | copy-start | bytes 95236
  3.6 0.7 %copy-start.3 = (s32[256]{0:T(256)S(1)}, s32[256]{0:T(256)}, u32[]{:S(2)}) copy-start(s32[256]{0:T(256)} %param.17) | copy-start | bytes 3076
  4.3 0.7 %copy-start.4 = (s32[128]{0:T(128)S(1)}, s32[128]{0:T(128)}, u32[]{:S(2)}) copy-start(s32[128]{0:T(128)} %param.12) | copy-start | bytes 1540
  5.0 0.7 %copy-start.5 = (s32[128]{0:T(128)S(1)}, s32[128]{0:T(128)}, u32[]{:S(2)}) copy-start(s32[128]{0:T(128)} %param.13) | copy-start | bytes 1540
  5.6 0.7 %copy-start.6 = (s32[128]{0:T(128)S(1)}, s32[128]{0:T(128)}, u32[]{:S(2)}) copy-start(s32[128]{0:T(128)} %param.14) | copy-start | bytes 1540

commit v3 on v2

--- a/solution.py
+++ b/solution.py
@@ -22,17 +22,22 @@
     scale,
     inverse_columns,
     count_ref,
-    source_ref,
-    tile_ref,
-    target_ref,
-    diffusivity_ref,
-    depth_ref,
+    source_hbm,
+    tile_hbm,
+    target_hbm,
+    diffusivity_hbm,
+    depth_hbm,
     flux_hbm,
     bank_hbm,
     tracers_hbm,
     mixed_ref,
     response_ref,
     forced_ref,
+    source_ref,
+    tile_ref,
+    target_ref,
+    diffusivity_ref,
+    depth_ref,
     flux,
     bank,
     tracers,
@@ -76,11 +81,27 @@
     def side_id(peer):
         return (peer // grp_count, lax.rem(peer, grp_count), blk)
 
+    small_copies = [
+        pltpu.make_async_copy(given_hbm, ref, local_sem.at[4 + i])
+        for i, (given_hbm, ref) in enumerate(
+            (
+                (target_hbm, target_ref),
+                (source_hbm, source_ref),
+                (tile_hbm, tile_ref),
+                (depth_hbm, depth_ref),
+                (diffusivity_hbm, diffusivity_ref),
+            )
+        )
+    ]
+    for small in small_copies[:3]:
+        small.start()
     flux_copy = pltpu.make_async_copy(flux_hbm, flux, local_sem.at[0])
     bank_copy = pltpu.make_async_copy(bank_hbm, bank, local_sem.at[1])
     tracers_copy = pltpu.make_async_copy(tracers_hbm, tracers, local_sem.at[2])
     flux_copy.start()
     bank_copy.start()
+    for small in small_copies[3:]:
+        small.start()
     tracers_copy.start()
 
     barrier = pltpu.get_barrier_semaphore()
@@ -95,6 +116,8 @@
 
     pairs = source_ref.shape[1]
     slots = lists.shape[1]
+    for small in small_copies[:3]:
+        small.wait()
     live_count = count_ref[0]
     square = (pairs, pairs)
     row_at = lax.broadcasted_iota(jnp.int32, square, 0)
@@ -214,6 +237,8 @@
         data_copy(line_peer(step), blk).start()
 
     fields, levels, columns = tracers.shape
+    for small in small_copies[3:]:
+        small.wait()
     depth = depth_ref[...]
     level_at = lax.broadcasted_iota(jnp.int32, (levels, columns), 0)
     wet = jnp.where(level_at < depth, 1.0, 0.0)
@@ -395,7 +420,6 @@
     slots = up(2 * steps_up, 128)
     f32, bf16 = jnp.float32, jnp.bfloat16
     vmem = pl.BlockSpec(memory_space=pltpu.VMEM)
-    smem = pl.BlockSpec(memory_space=pltpu.SMEM)
     anywhere = pl.BlockSpec(memory_space=pl.ANY)
     mixed, response, forced = pl.pallas_call(
         functools.partial(
@@ -412,9 +436,15 @@
             jax.ShapeDtypeStruct((2, levels, columns), f32),
             jax.ShapeDtypeStruct((subs, fields, columns), f32),
         ),
-        in_specs=[smem, vmem, vmem, vmem, vmem, vmem, anywhere, anywhere, anywhere],
+        in_specs=[pl.BlockSpec(memory_space=pltpu.SMEM)]
+        + [pl.BlockSpec(memory_space=pltpu.HBM)] * 8,
         out_specs=(vmem, vmem, vmem),
         scratch_shapes=[
+            pltpu.VMEM((1, pairs), jnp.int32),
+            pltpu.VMEM((1, pairs), jnp.int32),
+            pltpu.VMEM((1, pairs), jnp.int32),
+            pltpu.VMEM((levels - 1, columns), f32),
+            pltpu.VMEM((1, columns), jnp.int32),
             pltpu.VMEM((fields, subs, atm_rows), bf16),
             pltpu.VMEM(tile_bank.shape, bf16),
             pltpu.VMEM((fields, levels, columns), bf16),
@@ -435,7 +465,7 @@
             pltpu.VMEM((levels, columns), f32),
             pltpu.VMEM((levels, columns), f32),
             pltpu.VMEM((levels, columns), f32),
-            pltpu.SemaphoreType.DMA((5,)),
+            pltpu.SemaphoreType.DMA((9,)),
             pltpu.SemaphoreType.DMA((blk_count,)),
             pltpu.SemaphoreType.DMA((blk_count,)),
             pltpu.SemaphoreType.DMA((blk_count,)),
@@ -448,14 +478,19 @@
         ),
     )(
         pair_count,
-        pair_source.reshape(1, pairs),
-        pair_tile.reshape(1, pairs),
-        pair_target.reshape(1, pairs),
-        diffusivity,
-        column_depth.reshape(1, columns),
-        jnp.transpose(atm_flux, (1, 0, 2)),
-        tile_bank,
-        jnp.transpose(tracers, (1, 0, 2)),
+        *[
+            pltpu.with_memory_space_constraint(operand, pltpu.HBM)
+            for operand in (
+                pair_source.reshape(1, pairs),
+                pair_tile.reshape(1, pairs),
+                pair_target.reshape(1, pairs),
+                diffusivity,
+                column_depth.reshape(1, columns),
+                jnp.transpose(atm_flux, (1, 0, 2)),
+                tile_bank,
+                jnp.transpose(tracers, (1, 0, 2)),
+            )
+        ]
     )
     parts = 4 if fields % 4 == 0 else 1
     result = pl.pallas_call(

time: 26.1 us -> 20.2 us (0.77)
  local copies, waits for them, and re-layouts: 5.62 us -> 0 us
    unnamed x14 -> x0, local copies, waits for them, and re-layouts: 5.62 us -> none
where the time goes in v3:
time: 20.2 us; the launch traced here: 20.1 us
  Pallas kernels  19.4 us (96%)
  between operations  0.66 us (3%)
    pallas_call x1, Pallas kernels, body(): pl.pallas_call(functools.partial(couple_kernel, blk_count, grp_count, sid...  18 us
    pallas_call x1, Pallas kernels, body(): pl.pallas_call(functools.partial(join_kernel, parts), out_shape=jax.Shape...  1.46 us

profile of v3, /device:TPU:0, one launch (start us, length us, event | category | flops | bytes accessed | tf_op | source)
XLA Modules:
  0.0 20.1 jit_solution(18170142534154575448)
XLA Ops:
  0.7 18.0 %shard_map.91 = (f32[2,1920,128]{2,1,0:T(8,128)S(1)}, f32[2,32,256]{2,1,0:T(8,128)S(1)}, f32[2,60,256]{2,1,0:T(8,128)S(1)}) custom-call(s32[1]{0:T(128)S(6)} %copy.10.count_ref, s32[1,128]{1,0:T(1,128)} %bitcast.10, s32[1,128]{1,0:T(1,128)} %bitcast.11, s32[1,128]{1,0:T(1,128)} %bitcast.12, f32[31,256]{1,0:T(8,128)} %diffusivity_hbm.1, s32[1,256]{1,0:T(1,128)} %bitcast.9, ...), custom_call_target="tpu_custom_call" | custom-call | tf_op jit(solution)/shard_map/pallas_call | solution.py:424
  18.6 1.5 %shard_map.92 = f32[60,32,256]{2,1,0:T(8,128)} custom-call(f32[2,1920,128]{2,1,0:T(8,128)S(1)} %get-tuple-element.8.mixed_ref, f32[2,32,256]{2,1,0:T(8,128)S(1)} %get-tuple-element.9.response_ref, f32[2,60,256]{2,1,0:T(8,128)S(1)} %get-tuple-element.10.forced_ref), custom_call_target="tpu_custom_call" | custom-call | tf_op jit(solution)/shard_map/pallas_call | solution.py:496

commit v4 on v3

--- a/solution.py
+++ b/solution.py
@@ -181,7 +181,7 @@
         return total, target
 
     lax.fori_loop(
-        0, steps, add_step, (jnp.zeros((rows, width), jnp.float32), jnp.int32(-1)), unroll=4
+        0, steps, add_step, (jnp.zeros((rows, width), jnp.float32), jnp.int32(-1)), unroll=steps // 4
     )
 
     @pl.loop(0, blk_count)
@@ -245,32 +245,6 @@
     couple[0:1, :] = jnp.zeros((1, columns), jnp.float32)
     couple[1:levels, :] = diffusivity_ref[...] * wet[1:levels]
     couple[levels : levels + 1, :] = jnp.zeros((1, columns), jnp.float32)
-    previous = jnp.zeros((1, columns), jnp.float32)
-    for k in range(levels):
-        a = couple[k : k + 1, :]
-        b = couple[k + 1 : k + 2, :]
-        inverse = 1.0 / (1.0 + a + b - a * previous)
-        previous = b * inverse
-        weight[k : k + 1, :] = jnp.where(depth > k, inverse, 0.0)
-        carry[k : k + 1, :] = a * inverse
-        ratio[k : k + 1, :] = previous
-    for sweep in range(2):
-        right = response_ref.at[0]
-        unit = jnp.zeros((1, columns), jnp.float32)
-        forward = []
-        for k in range(levels):
-            if sweep == 0:
-                pushed = weight[0:1, :] if k == 0 else jnp.zeros((1, columns), jnp.float32)
-            else:
-                pushed = right[k : k + 1, :] * weight[k : k + 1, :]
-            unit = pushed + carry[k : k + 1, :] * unit
-            forward.append(unit)
-        solved = forward[-1]
-        response_ref[sweep, levels - 1 : levels, :] = solved
-        for k in range(levels - 2, -1, -1):
-            solved = forward[k] + ratio[k : k + 1, :] * solved
-            response_ref[sweep, k : k + 1, :] = solved
-
     tracers_copy.wait()
 
     @pl.loop(0, fields)
@@ -288,30 +262,59 @@
             mixed_ref[o, level_rows(k), :] = held[:, o * width : (o + 1) * width]
 
     def first_level(k, held):
+        state_row, unit, previous = held
+        at = pl.ds(k, 1)
+        below, above = couple[at, :], couple[pl.ds(k + 1, 1), :]
+        inverse = 1.0 / (1.0 + below + above - below * previous)
+        previous = above * inverse
+        kept = jnp.where(depth > k, inverse, 0.0)
+        passed = below * inverse
+        weight[at, :], carry[at, :], ratio[at, :] = kept, passed, previous
         read = [given[o, level_rows(k), :] for o in range(ocean_blocks)]
-        held = jnp.concatenate(read, axis=1) * weight[pl.ds(k, 1), :] + carry[pl.ds(k, 1), :] * held
-        state[k] = held
-        return held
+        state_row = jnp.concatenate(read, axis=1) * kept + passed * state_row
+        state[k] = state_row
+        unit = jnp.where(k == 0, kept, 0.0) + passed * unit
+        response_ref[0, at, :] = unit
+        return state_row, unit, previous
 
     def forward_level(k, held):
-        held = state[k] * weight[pl.ds(k, 1), :] + carry[pl.ds(k, 1), :] * held
-        state[k] = held
-        return held
-
-    def back_level(i, held):
-        k = levels - 2 - i
-        held = state[k] + ratio[pl.ds(k, 1), :] * held
-        state[k] = held
-        return held
-
-    def last_level(i, held):
-        k = levels - 2 - i
-        held = state[k] + ratio[pl.ds(k, 1), :] * held
-        put_level(k, held)
-        return held
-
+        state_row, unit = held
+        at = pl.ds(k, 1)
+        kept, passed = weight[at, :], carry[at, :]
+        state_row = state[k] * kept + passed * state_row
+        state[k] = state_row
+        unit = response_ref[0, at, :] * kept + passed * unit
+        response_ref[1, at, :] = unit
+        return state_row, unit
+
+    def back_level(k, held):
+        state_row, unit = held
+        at = pl.ds(k, 1)
+        share = ratio[at, :]
+        state_row = state[k] + share * state_row
+        state[k] = state_row
+        unit = response_ref[0, at, :] + share * unit
+        response_ref[0, at, :] = unit
+        return state_row, unit
+
+    def last_level(k, held):
+        state_row, unit = held
+        at = pl.ds(k, 1)
+        share = ratio[at, :]
+        state_row = state[k] + share * state_row
+        put_level(k, state_row)
+        unit = response_ref[1, at, :] + share * unit
+        response_ref[1, at, :] = unit
+        return state_row, unit
+
+    def go_back(level, held):
+        held = level(levels - 2, held)
+        unroll = 5 if (levels - 2) % 5 == 0 else 1
+        lax.fori_loop(0, levels - 2, lambda i, h: level(levels - 3 - i, h), held, unroll=unroll)
+
+    no_row = jnp.zeros((1, columns), jnp.float32)
     nothing = jnp.zeros((fields, columns), jnp.float32)
-    bottom = lax.fori_loop(0, levels, first_level, nothing, unroll=4)
+    bottom = lax.fori_loop(0, levels, first_level, (nothing, no_row, no_row), unroll=4)[:2]
 
     @pl.loop(1, blk_count)
     def _(step):
@@ -327,10 +330,10 @@
     def _(step):
         side_copy(side_peer(step), side).start()
 
-    lax.fori_loop(0, levels - 1, back_level, bottom)
-    bottom = lax.fori_loop(0, levels, forward_level, nothing, unroll=4)
-    put_level(levels - 1, bottom)
-    lax.fori_loop(0, levels - 1, last_level, bottom)
+    go_back(back_level, bottom)
+    bottom = lax.fori_loop(0, levels, forward_level, (nothing, no_row), unroll=4)
+    put_level(levels - 1, bottom[0])
+    go_back(last_level, bottom)
 
     @pl.loop(1, side_count)
     def _(step):
@@ -380,15 +383,12 @@
         return pltpu.make_async_copy(result.at[at], result_hbm.at[at], sems.at[n])
 
     for n in range(parts):
-
-        @pl.loop(n * part, (n + 1) * part)
-        def _(f):
-            at = pl.ds(pl.multiple_of(f * levels, levels), levels)
+        for f in range(n * part, (n + 1) * part):
+            at = slice(f * levels, (f + 1) * levels)
             mixed = jnp.concatenate([mixed_ref[o, at, :] for o in range(halves)], axis=1)
-            early = forced_ref[0, pl.ds(f, 1), :]
-            late = forced_ref[1, pl.ds(f, 1), :]
+            early = forced_ref[0, f : f + 1, :]
+            late = forced_ref[1, f : f + 1, :]
             result[f] = mixed + far * early + near * late
-
         copy(n).start()
     for n in range(parts):
         copy(n).wait()
@@ -492,7 +492,7 @@
             )
         ]
     )
-    parts = 4 if fields % 4 == 0 else 1
+    parts = 10 if fields % 10 == 0 else 1
     result = pl.pallas_call(
         functools.partial(join_kernel, parts),
         out_shape=jax.ShapeDtypeStruct((fields, levels, columns), f32),

time: 20.2 us -> 18.1 us (0.90)
  Pallas kernels: 19.4 us -> 17.3 us
    pallas_call x1, Pallas kernels: 18 us -> 15.9 us  [body(): pl.pallas_call(functools.partial(couple_kernel, blk_count, grp_count, sid...]
where the time goes in v4:
time: 18.1 us; the launch traced here: 18 us
  Pallas kernels  17.3 us (96%)
  between operations  0.66 us (4%)
    pallas_call x1, Pallas kernels, body(): pl.pallas_call(functools.partial(couple_kernel, blk_count, grp_count, sid...  15.9 us
    pallas_call x1, Pallas kernels, body(): pl.pallas_call(functools.partial(join_kernel, parts), out_shape=jax.Shape...  1.38 us

profile of v4, /device:TPU:0, one launch (start us, length us, event | category | flops | bytes accessed | tf_op | source)
XLA Modules:
  0.0 18.0 jit_solution(16995024381626122337)
XLA Ops:
  0.7 15.9 %shard_map.91 = (f32[2,1920,128]{2,1,0:T(8,128)S(1)}, f32[2,32,256]{2,1,0:T(8,128)S(1)}, f32[2,60,256]{2,1,0:T(8,128)S(1)}) custom-call(s32[1]{0:T(128)S(6)} %copy.10.count_ref, s32[1,128]{1,0:T(1,128)} %bitcast.10, s32[1,128]{1,0:T(1,128)} %bitcast.11, s32[1,128]{1,0:T(1,128)} %bitcast.12, f32[31,256]{1,0:T(8,128)} %diffusivity_hbm.1, s32[1,256]{1,0:T(1,128)} %bitcast.9, ...), custom_call_target="tpu_custom_call" | custom-call | tf_op jit(solution)/shard_map/pallas_call | solution.py:424
  16.6 1.4 %shard_map.92 = f32[60,32,256]{2,1,0:T(8,128)} custom-call(f32[2,1920,128]{2,1,0:T(8,128)S(1)} %get-tuple-element.8.mixed_ref, f32[2,32,256]{2,1,0:T(8,128)S(1)} %get-tuple-element.9.response_ref, f32[2,60,256]{2,1,0:T(8,128)S(1)} %get-tuple-element.10.forced_ref), custom_call_target="tpu_custom_call" | custom-call | tf_op jit(solution)/shard_map/pallas_call | solution.py:496

commit v5 on v4

--- a/solution.py
+++ b/solution.py
@@ -59,6 +59,7 @@
     carry,
     ratio,
     local_sem,
+    bank_sem,
     send_sem,
     recv_sem,
     line_send,
@@ -96,10 +97,19 @@
     for small in small_copies[:3]:
         small.start()
     flux_copy = pltpu.make_async_copy(flux_hbm, flux, local_sem.at[0])
-    bank_copy = pltpu.make_async_copy(bank_hbm, bank, local_sem.at[1])
+    bank_part = bank.shape[0] // bank_sem.shape[0]
+    bank_copies = [
+        pltpu.make_async_copy(
+            bank_hbm.at[pl.ds(n * bank_part, bank_part)],
+            bank.at[pl.ds(n * bank_part, bank_part)],
+            bank_sem.at[n],
+        )
+        for n in range(bank_sem.shape[0])
+    ]
     tracers_copy = pltpu.make_async_copy(tracers_hbm, tracers, local_sem.at[2])
     flux_copy.start()
-    bank_copy.start()
+    for part in bank_copies:
+        part.start()
     for small in small_copies[3:]:
         small.start()
     tracers_copy.start()
@@ -167,7 +177,8 @@
     own_total[...] = spread * scale
 
     lists_copy.wait()
-    bank_copy.wait()
+    for part in bank_copies:
+        part.wait()
 
     def add_step(step, held):
         total, last = held
@@ -181,7 +192,7 @@
         return total, target
 
     lax.fori_loop(
-        0, steps, add_step, (jnp.zeros((rows, width), jnp.float32), jnp.int32(-1)), unroll=steps // 4
+        0, steps, add_step, (jnp.zeros((rows, width), jnp.float32), jnp.int32(-1)), unroll=steps // 2
     )
 
     @pl.loop(0, blk_count)
@@ -234,7 +245,15 @@
 
     @pl.loop(1, blk_count)
     def _(step):
-        data_copy(line_peer(step), blk).start()
+        distance = blk_count - step
+
+        @pl.when(blk + distance < blk_count)
+        def _():
+            data_copy(blk + distance, blk).start()
+
+        @pl.when(blk >= distance)
+        def _():
+            data_copy(blk - distance, blk).start()
 
     fields, levels, columns = tracers.shape
     for small in small_copies[3:]:
@@ -466,6 +485,7 @@
             pltpu.VMEM((levels, columns), f32),
             pltpu.VMEM((levels, columns), f32),
             pltpu.SemaphoreType.DMA((9,)),
+            pltpu.SemaphoreType.DMA((8 if tile_bank.shape[0] % 8 == 0 else 1,)),
             pltpu.SemaphoreType.DMA((blk_count,)),
             pltpu.SemaphoreType.DMA((blk_count,)),
             pltpu.SemaphoreType.DMA((blk_count,)),

time: 18.1 us -> 17.8 us (0.983)
  Pallas kernels: 17.3 us -> 17 us
    pallas_call x1, Pallas kernels: 15.9 us -> 15.7 us  [body(): pl.pallas_call(functools.partial(couple_kernel, blk_count, grp_count, sid...]
where the time goes in v5:
time: 17.8 us; the launch traced here: 17.7 us
  Pallas kernels  17 us (96%)
  between operations  0.66 us (4%)
    pallas_call x1, Pallas kernels, body(): pl.pallas_call(functools.partial(couple_kernel, blk_count, grp_count, sid...  15.7 us
    pallas_call x1, Pallas kernels, body(): pl.pallas_call(functools.partial(join_kernel, parts), out_shape=jax.Shape...  1.38 us

profile of v5, /device:TPU:0, one launch (start us, length us, event | category | flops | bytes accessed | tf_op | source)
XLA Modules:
  0.0 17.7 jit_solution(5058227590594910961)
XLA Ops:
  0.7 15.7 %shard_map.91 = (f32[2,1920,128]{2,1,0:T(8,128)S(1)}, f32[2,32,256]{2,1,0:T(8,128)S(1)}, f32[2,60,256]{2,1,0:T(8,128)S(1)}) custom-call(s32[1]{0:T(128)S(6)} %copy.10.count_ref, s32[1,128]{1,0:T(1,128)} %bitcast.10, s32[1,128]{1,0:T(1,128)} %bitcast.11, s32[1,128]{1,0:T(1,128)} %bitcast.12, f32[31,256]{1,0:T(8,128)} %diffusivity_hbm.1, s32[1,256]{1,0:T(1,128)} %bitcast.9, ...), custom_call_target="tpu_custom_call" | custom-call | tf_op jit(solution)/shard_map/pallas_call | solution.py:443
  16.3 1.4 %shard_map.92 = f32[60,32,256]{2,1,0:T(8,128)} custom-call(f32[2,1920,128]{2,1,0:T(8,128)S(1)} %get-tuple-element.8.mixed_ref, f32[2,32,256]{2,1,0:T(8,128)S(1)} %get-tuple-element.9.response_ref, f32[2,60,256]{2,1,0:T(8,128)S(1)} %get-tuple-element.10.forced_ref), custom_call_target="tpu_custom_call" | custom-call | tf_op jit(solution)/shard_map/pallas_call | solution.py:516
